TPU v7x, 256 devices: a whole 4x4x8 slice. The times are simulated.
256 devices in a mesh: space: 128 (over x, y, z), blk: 2 (over core).
Axes of the slice: x: 4, y: 4, z: 8, core: 2. Of those that a mesh axis runs over, the one named last changes fastest.
Arguments:
- spectra: bfloat16 [4, 2, 64, 1048576], P(None, None, 'blk', 'space'), may hold values from -1600 to 1600
- weights: float32 [1048576], P('space'), may hold values from 0 to 0.00019073486, as said below
- vectors: float32 [4, 2, 64, 8], replicated, may hold values from -0.5 to 0.5
Outputs:
- gram: float32 [4, 2, 64, 64], replicated
- modes: bfloat16 [4, 2, 8, 1048576], P(None, None, None, ('space', 'blk'))
Inputs may be any that keep to these rules, and one draw needn't show every extreme that they name: `weights`: positive.
All inputs are finite; a program needn't handle non-finite values.
Results may differ from a plain program's by a relative error of at most 0.0052.
Values may be sent and summed in bfloat16 or wider, within the bound.
A program may use at most 128 MiB of HBM per device.

v0:
```python
import jax
import jax.numpy as jnp
from jax import lax
from jax.sharding import PartitionSpec as P

K = 4
M = 64


def on_device(spectra, weights, vectors):
    hp = lax.Precision.HIGHEST
    count_blk = lax.axis_size("blk")
    points = spectra.shape[3]
    share = points // count_blk
    offset = lax.axis_index("blk") * share
    blocks_all = lax.all_gather(spectra, "blk", axis=2, tiled=True)
    for_modes = lax.dynamic_slice_in_dim(blocks_all, offset, share, 3)
    width = blocks_all.shape[3]
    stacked = blocks_all.reshape(K, 2 * M, width)
    partials = []
    for k in range(K):
        weighted = (stacked[k].astype(jnp.float32) * weights[None, :]).astype(jnp.bfloat16)
        partials.append(
            lax.dot_general(
                weighted, stacked[k], (((1,), (1,)), ((), ())), preferred_element_type=jnp.float32
            )
        )
    partial_all = jnp.stack(partials)
    psi_b = vectors.astype(jnp.bfloat16)
    upper = jnp.concatenate([psi_b[:, 0], -psi_b[:, 1]], axis=1)
    lower = jnp.concatenate([psi_b[:, 1], psi_b[:, 0]], axis=1)
    mixers = jnp.stack([upper, lower], axis=1)
    mode_rows = for_modes.reshape(K, 2 * M, share)
    raw = jnp.einsum("kcmn,kmp->kcnp", mixers, mode_rows, preferred_element_type=jnp.float32)
    products = lax.psum(partial_all, "space")
    real_part = (products[:, :M, :M] + products[:, M:, M:]) / M
    imag_part = (products[:, :M, M:] - products[:, M:, :M]) / M
    gram = jnp.stack([real_part, imag_part], axis=1)
    vec_re = vectors[:, 0]
    vec_im = vectors[:, 1]
    prod_re = jnp.einsum("kab,kbn->kan", real_part, vec_re, precision=hp) - jnp.einsum(
        "kab,kbn->kan", imag_part, vec_im, precision=hp
    )
    prod_im = jnp.einsum("kab,kbn->kan", real_part, vec_im, precision=hp) + jnp.einsum(
        "kab,kbn->kan", imag_part, vec_re, precision=hp
    )
    lam = jnp.sum(vec_re * prod_re + vec_im * prod_im, axis=1)
    factor = lax.rsqrt(lam + 1e-06)[:, None, :, None]
    modes = (raw * factor).astype(jnp.bfloat16)
    return (gram, modes)


def solution(mesh):
    placed = (P(None, None, "blk", "space"), P("space"), P())
    return jax.shard_map(
        on_device,
        mesh=mesh,
        in_specs=placed,
        out_specs=(P(), P(None, None, None, ("space", "blk"))),
        check_vma=False,
    )
```

profile of v0, /device:TPU:1, one launch (start us, length us, event | category | flops | bytes accessed | tf_op | source)
XLA Modules:
  0.0 278.4 jit_solution(10284551817012195025)
XLA Ops:
  7.2 0.0 copy-start.1
  7.2 0.0 all-gather.2.cloned.1.call-start
  7.2 0.7 all-gather.2.cloned.1.call-update
  7.9 0.0 all-reduce.2.cloned.1.call-start
  8.0 0.1 maximum_bitcast_fusion
  8.1 31.5 %all-gather.2.cloned.1.call-done = bf16[4,2,64,8192]{3,2,1,0:T(8,128)(2,1)} async-done(((bf16[4,2,32,8192]{3,2,1,0:T(8,128)(2,1)}), bf16[4,2,64,8192]{3,2,1,0:T(8,128)(2,1)}) %all-gather.2.cloned.1.call-update) | async-done | bytes 8388624 | tf_op jit(solution)/shard_map/all_gather | solution.py:16
  39.6 4.0 %fusion.20 = (bf16[1,2,64,8192]{3,2,1,0:T(8,128)(2,1)S(1)}, bf16[1,2,64,8192]{3,2,1,0:T(8,128)(2,1)S(1)}, bf16[1,2,64,8192]{3,2,1,0:T(8,128)(2,1)S(1)}, bf16[1,2,64,8192]{3,2,1,0:T(8,128)(2,1)S(1)}) fusion(bf16[4,2,64,8192]{3,2,1,0:T(8,128)(2,1)} %all-gather.2.cloned.1.call-done), kind=kLoop, calls=%fused_computation.40 | loop fusion | bytes 16777216 | tf_op jit(solution)/shard_map/slice | solution.py:22
  43.6 1.8 copy-done
  45.4 2.2 multiply_convert_fusion.3
  47.6 0.7 convolution_bitcast_fusion.1
  48.3 0.7 convolution_bitcast_fusion.2
  49.0 0.7 convolution_bitcast_fusion.3
  49.8 0.7 convolution_bitcast_fusion
  50.5 0.7 pad_maximum_fusion
  51.2 0.0 all-reduce.2.cloned.1.call-update
  51.2 4.7 %constant_dynamic-slice_fusion = bf16[4,2,64,4096]{3,2,1,0:T(8,128)(2,1)} fusion(bf16[4,2,64,8192]{3,2,1,0:T(8,128)(2,1)} %all-gather.2.cloned.1.call-done, s32[]{:T(128)S(6)} %select_n.3), kind=kLoop, calls=%fused_computation.34 | loop fusion | bytes 8388612 | tf_op jit(solution)/shard_map/dynamic_slice | solution.py:17
  55.9 204.4 %all-reduce.2.cloned.1.call-done = f32[4,128,128]{2,1,0:T(8,128)} async-done(((f32[4,128,128]{2,1,0:T(8,128)}), f32[4,128,128]{2,1,0:T(8,128)}) %all-reduce.2.cloned.1.call-update) | async-done | bytes 262160 | tf_op jit(solution)/shard_map/psum | solution.py:35
  260.3 1.4 fusion.10
  261.6 1.4 fusion.11
  263.0 1.4 fusion.3
  264.4 1.5 fusion.4
  265.9 1.3 fusion.16
  267.2 0.7 copy.9
  267.9 3.6 %fusion = bf16[4,2,8,4096]{3,2,1,0:T(8,128)(2,1)} fusion(bf16[4,128,4096,1]{2,1,3,0:T(8,128)(2,1)} %bitcast.58, f32[4,8]{1,0:T(4,128)S(1)} %add_rsqrt_fusion, bf16[4,1,128,8]{2,3,1,0:T(8,128)(2,1)S(1)} %get-tuple-element.17, bf16[4,1,128,8]{2,3,1,0:T(8,128)(2,1)S(1)} %get-tuple-element.16), kind=kOutput, calls=%fused_computation.1 | convolution fusion | flops 67641344 | bytes 4735104 | tf_op jit(solution)/shard_map/kcmn,kmp->kcnp/dot_general | solution.py:34
  (8 shorter events, 0.0 us)
Async XLA Ops:
  7.2 0.8 copy-start.1
  7.2 32.4 %all-gather.2.cloned.1.call-start = ((), (), s32[]{:S(2)}) async-start(), calls=%async_computation | async-start | bytes 12582912 | tf_op jit(solution)/shard_map/all_gather | solution.py:16
  7.9 252.4 %all-reduce.2.cloned.1.call-start = ((), (), s32[]{:S(2)}) async-start(), calls=%async_computation.1 | async-start | bytes 524288 | tf_op jit(solution)/shard_map/psum | solution.py:35
  8.1 35.5 %copy-start.2 = (f32[8192]{0:T(1024)S(1)}, f32[8192]{0:T(1024)}, u32[]{:S(2)}) copy-start(f32[8192]{0:T(1024)} %param.4) | copy-start | bytes 98308
  39.6 5.9 %copy-start = (bf16[4,2,64,8192]{3,2,1,0:T(8,128)(2,1)S(1)}, bf16[4,2,64,8192]{3,2,1,0:T(8,128)(2,1)}, u32[]{:S(2)}) copy-start(bf16[4,2,64,8192]{3,2,1,0:T(8,128)(2,1)} %all-gather.2.cloned.1.call-done) | copy-start | bytes 25165828
Sparse Core Ops, SparseCore 0:
  9.8 29.7 all-gather.1
  51.3 208.9 all-reduce.1
where the time goes:
time: 282 us; the launch traced here: 278 us
  waiting for transfers between devices  237 us (84%)
  between operations  14.1 us (5%)
  matrix products  12 us (4%)
  local copies, waits for them, and re-layouts  11.2 us (4%)
  other arithmetic  4.29 us (2%)
    psum x1, waiting for transfers between devices, on_device(): products = lax.psum(partial_all, 'space')  204 us
    all_gather x1, waiting for transfers between devices, on_device(): blocks_all = lax.all_gather(spectra, 'blk', axis=2, tiled=True)  31.5 us
  transfers between devices with their start and end apart: 2, of which 2 were waited for; matrix products, arithmetic and copies ran while one was open for 2% of the time, Pallas kernels for 0%

commit v1 on v0

v1 whole, which is shorter than its diff:
```python
import jax
import jax.numpy as jnp
from jax import lax
from jax.experimental import pallas as pl
from jax.experimental.pallas import tpu as pltpu
from jax.sharding import PartitionSpec as P

MESH = pl.DeviceIdType.MESH
K, M, N = 4, 64, 8
NX, NY, NZ = 4, 4, 8
PLANE = NX * NY
BINS = K // 2
HALF = M // 2
ROWS = 48
CHUNKS = 2
TILE = 1024
XY, Z = 0, 1


def ring_distance(d, n):
    return min(d, n - d)


STEPS_XY = sorted(
    ((dx, dy) for dx in range(NX) for dy in range(NY) if dx or dy),
    key=lambda d: -ring_distance(d[0], NX) - ring_distance(d[1], NY),
)
STEPS_Z = sorted(range(1, NZ), key=lambda d: -ring_distance(d, NZ))


def kernel(
    spec, wts, vec, gram, modes,
    s_all, w, v, mix, raw, box_xy, box_z, gram_out, modes_out,
    pair, all_in, load_sem, small_sem, swap_send, swap_recv, sum_send, sum_recv, out_sem, out_send, out_recv,
):
    here = lax.axis_index("space")
    core = lax.axis_index("blk")
    x, y, z = here // (NY * NZ), (here // NZ) % NY, here % NZ
    points = s_all.shape[3]
    span = points // CHUNKS
    share = points // 2
    sibling = (here, 1 - core)
    first = core * BINS
    peers = {
        XY: [((((x + dx) % NX) * NY + (y + dy) % NY) * NZ + z, core) for dx, dy in STEPS_XY],
        Z: [((x * NY + y) * NZ + (z + d) % NZ, core) for d in STEPS_Z],
    }
    boxes = {XY: box_xy, Z: box_z}
    slots = {XY: x * NY + y, Z: z}

    w_copy = pltpu.make_async_copy(wts, w, small_sem.at[0])
    v_copy = pltpu.make_async_copy(vec.at[pl.ds(first, BINS)], v, small_sem.at[1])
    v_copy.start()
    w_copy.start()
    rows = pl.ds(pl.multiple_of(core * HALF, HALF), HALF)
    loads, swaps = {}, {}
    for k in range(BINS):
        for h in range(CHUNKS):
            cols = pl.ds(h * span, span)
            loads[k, h] = pltpu.make_async_copy(
                spec.at[first + k, :, :, cols], s_all.at[k, :, rows, cols], load_sem.at[k, h]
            )
            swaps[k, h] = pltpu.make_async_remote_copy(
                src_ref=spec.at[BINS - first + k, :, :, cols],
                dst_ref=s_all.at[k, :, rows, cols],
                send_sem=swap_send.at[k, h],
                recv_sem=swap_recv.at[k, h],
                device_id=sibling,
                device_id_type=MESH,
            )

    barrier = pltpu.get_barrier_semaphore()

    @pl.when(core == 1)
    def _():
        pl.semaphore_signal(barrier, inc=1, device_id=(here, 0), device_id_type=MESH)

    @pl.when(core == 0)
    def _():
        pl.semaphore_wait(barrier, 1)
        pl.semaphore_signal(pair, inc=1, device_id=(here, 1), device_id_type=MESH)

    @pl.when(core == 1)
    def _():
        pl.semaphore_wait(pair, 1)

    for k in range(BINS):
        for h in range(CHUNKS):
            swaps[k, h].start()
            loads[k, h].start()

    @pl.when(core == 1)
    def _():
        for t, _ in peers[XY] + peers[Z]:
            pl.semaphore_signal(barrier, inc=1, device_id=(t, 1), device_id_type=MESH)

    v_copy.wait()
    for k in range(BINS):
        re, im = v[k, 0], v[k, 1]
        both = jnp.concatenate(
            [jnp.concatenate([re, -im], axis=1), jnp.concatenate([im, re], axis=1)], axis=0
        )
        high = both.astype(jnp.bfloat16).astype(jnp.float32)
        mix[k] = jnp.concatenate([high, both - high], axis=0).astype(jnp.bfloat16)
    w_copy.wait()

    def products(k):
        total = jnp.zeros((2 * M, 2 * M), jnp.float32)
        power = jnp.zeros((N, 128), jnp.float32)
        mixer = mix[k]
        for h in range(CHUNKS):
            loads[k, h].wait()
            swaps[k, h].wait_recv()

            def step(i, carry):
                total, power = carry
                cols = pl.ds(pl.multiple_of(h * span + i * TILE, TILE), TILE)
                s = s_all[k, :, :, cols].reshape(2 * M, TILE)
                wt = w[:, cols]
                weighted = (s.astype(jnp.float32) * wt).astype(jnp.bfloat16)
                total += lax.dot_general(
                    weighted, s, (((1,), (1,)), ((), ())), preferred_element_type=jnp.float32
                )
                r = jnp.dot(mixer, s, preferred_element_type=jnp.float32)
                raw[k, :, cols] = r[: 2 * N]
                full = r[: 2 * N] + r[2 * N :]
                square = full * full
                square = (square[:N] + square[N:]) * wt
                for g in range(TILE // 128):
                    power += square[:, g * 128 : (g + 1) * 128]
                return total, power

            total, power = lax.fori_loop(0, span // TILE, step, (total, power))
        return total, power

    row = lax.broadcasted_iota(jnp.int32, (M, 128), 0)
    lane = lax.broadcasted_iota(jnp.int32, (M, 128), 1)

    def message(packed, power):
        high = power.astype(jnp.bfloat16).astype(jnp.float32)
        return jnp.concatenate([packed, high, power - high], axis=0).astype(jnp.bfloat16)

    def pack(total):
        turned = pltpu.roll(total, M, 1)
        real = total[:M] + turned[M:]
        imag = turned[:M] - total[M:]
        held = jnp.where(row >= lane, real, imag)
        return jnp.where(lane[:HALF] < M, held[:HALF], pltpu.roll(held, M, 1)[HALF:])

    def send(k, axis, what):
        box = boxes[axis].at[k, slots[axis]]
        box[...] = what
        for t in peers[axis]:
            pltpu.make_async_remote_copy(
                src_ref=box,
                dst_ref=box,
                send_sem=sum_send.at[k, axis],
                recv_sem=sum_recv.at[k, axis],
                device_id=t,
                device_id_type=MESH,
            ).start()

    def all_others(k, axis):
        return boxes[axis].at[k, pl.ds(0, len(peers[axis]))]

    def gather(k, axis):
        ref = all_others(k, axis)
        pltpu.make_async_copy(ref, ref, sum_recv.at[k, axis]).wait()
        got = boxes[axis][k].astype(jnp.float32)
        got = jnp.sum(got, axis=0)
        return got[:HALF], got[HALF : HALF + N] + got[HALF + N :]

    outs = []

    def finish(k, packed, power):
        lam = jnp.sum(power, axis=1, keepdims=True) / M
        factor = lax.rsqrt(lam + 1e-06)
        factor = jnp.concatenate([factor, factor], axis=0)
        modes_out[k] = (raw[k] * factor).astype(jnp.bfloat16)
        own = modes_out.at[k, :, pl.ds(pl.multiple_of(core * share, share), share)]
        other = modes_out.at[k, :, pl.ds(pl.multiple_of((1 - core) * share, share), share)]
        put(2 * k, own, other, modes.at[first + k])
        packed = packed / M
        held = jnp.concatenate([packed, pltpu.roll(packed, M, 1)], axis=0)
        across = jnp.concatenate([held, held], axis=0).T[:M]
        real = jnp.where(row >= lane, held, across)
        imag = jnp.where(row < lane, held, jnp.where(row > lane, -across, 0.0))
        gram_out[k, 0] = real[:, :M]
        gram_out[k, 1] = imag[:, :M]
        put(2 * k + 1, gram_out.at[k], gram_out.at[k], gram.at[first + k])

    def put(i, own, other, target):
        away = pltpu.make_async_remote_copy(
            src_ref=other,
            dst_ref=target,
            send_sem=out_send.at[i],
            recv_sem=out_recv.at[i],
            device_id=sibling,
            device_id_type=MESH,
        )
        home = pltpu.make_async_copy(own, target, out_sem.at[i])
        away.start()
        home.start()
        outs.append((away, home))

    total, power = products(0)

    @pl.when(core == 1)
    def _():
        pl.semaphore_wait(barrier, len(STEPS_XY) + len(STEPS_Z))
        pl.semaphore_signal(all_in, inc=1, device_id=(here, 0), device_id_type=MESH)

    @pl.when(core == 0)
    def _():
        pl.semaphore_wait(all_in, 1)

    send(0, XY, message(pack(total), power))
    total, power = products(1)
    send(1, Z, message(pack(total), power))
    send(0, Z, message(*gather(0, XY)))
    send(1, XY, message(*gather(1, Z)))
    finish(0, *gather(0, Z))
    finish(1, *gather(1, XY))

    for k in range(BINS):
        for h in range(CHUNKS):
            swaps[k, h].wait_send()
        for axis in (XY, Z):
            ref = all_others(k, axis)
            pltpu.make_async_copy(ref, ref, sum_send.at[k, axis]).wait()
    for away, home in outs:
        away.wait()
        home.wait()


def on_device(spectra, weights, vectors):
    points = spectra.shape[3]
    dma = pltpu.SemaphoreType.DMA
    gram, modes = pl.pallas_call(
        kernel,
        out_shape=(
            jax.ShapeDtypeStruct((K, 2, M, M), jnp.float32),
            jax.ShapeDtypeStruct((K, 2 * N, points // 2), jnp.bfloat16),
        ),
        in_specs=[pl.BlockSpec(memory_space=pl.ANY)] * 3,
        out_specs=[pl.BlockSpec(memory_space=pl.ANY)] * 2,
        scratch_shapes=[
            pltpu.VMEM((BINS, 2, M, points), jnp.bfloat16),
            pltpu.VMEM((1, points), jnp.float32),
            pltpu.VMEM((BINS, 2, N, M), jnp.float32),
            pltpu.VMEM((BINS, 4 * N, 2 * M), jnp.bfloat16),
            pltpu.VMEM((BINS, 2 * N, points), jnp.float32),
            pltpu.VMEM((BINS, PLANE, ROWS, 128), jnp.bfloat16),
            pltpu.VMEM((BINS, NZ, ROWS, 128), jnp.bfloat16),
            pltpu.VMEM((BINS, 2, M, M), jnp.float32),
            pltpu.VMEM((BINS, 2 * N, points), jnp.bfloat16),
            pltpu.SemaphoreType.REGULAR,
            pltpu.SemaphoreType.REGULAR,
            dma((BINS, CHUNKS)),
            dma((2,)),
            dma((BINS, CHUNKS)),
            dma((BINS, CHUNKS)),
            dma((BINS, 2)),
            dma((BINS, 2)),
            dma((2 * BINS,)),
            dma((2 * BINS,)),
            dma((2 * BINS,)),
        ],
        compiler_params=pltpu.CompilerParams(
            collective_id=0, has_side_effects=True, vmem_limit_bytes=56 * 1024 * 1024
        ),
    )(spectra, weights.reshape(1, points), jnp.swapaxes(vectors, 2, 3))
    return gram, modes.reshape(K, 2, N, points // 2)


def solution(mesh):
    return jax.shard_map(
        on_device,
        mesh=mesh,
        in_specs=(P(None, None, "blk", "space"), P("space"), P()),
        out_specs=(P(), P(None, None, None, ("space", "blk"))),
        check_vma=False,
    )
```

time: 282 us -> 31.2 us (0.11); the launches traced: 278 us -> 31 us
  waiting for transfers between devices: 237 us -> 0 us
  Pallas kernels: 0 us -> 26.8 us
  between operations: 14.1 us -> 0.64 us
  matrix products: 12 us -> 0 us
  local copies, waits for them, and re-layouts: 11.2 us -> 3.54 us
  other arithmetic: 4.29 us -> 0 us
    psum x1 -> x0, waiting for transfers between devices: 204 us -> none  [on_device(): products = lax.psum(partial_all, 'space')]
    all_gather x1 -> x0, waiting for transfers between devices: 31.5 us -> none  [on_device(): blocks_all = lax.all_gather(spectra, 'blk', axis=2, tiled=True)]
    pallas_call x0 -> x1, Pallas kernels: none -> 26.8 us  [on_device(): pl.pallas_call(kernel, out_shape=(jax.ShapeDtypeStruct((K, 2, M, M), jnp....]
    dot_general x9 -> x0, matrix products: 12 us -> none  [the longest x1 3.64 us: on_device(): jnp.einsum('kcmn,kmp->kcnp', mixers, mode_rows, preferred_element_type=jn...]
    dynamic_slice x1 -> x0, local copies, waits for them, and re-layouts: 4.65 us -> none  [on_device(): for_modes = lax.dynamic_slice_in_dim(blocks_all, offset, share, 3)]
    slice x1 -> x0, local copies, waits for them, and re-layouts: 4.03 us -> none  [on_device(): stacked[k].astype(jnp.float32) * weights[None, :]]
  transfers between devices with their start and end apart: 2 -> 0, of which waited for: 2 -> 0; matrix products, arithmetic and copies ran while one was open for 2% -> 0% of each run, Pallas kernels for 0% -> 0%
where the time goes in v1:
time: 31.2 us; the launch traced here: 31 us
  Pallas kernels  26.8 us (86%)
  local copies, waits for them, and re-layouts  3.54 us (11%)
  between operations  0.64 us (2%)
    pallas_call x1, Pallas kernels, on_device(): pl.pallas_call(kernel, out_shape=(jax.ShapeDtypeStruct((K, 2, M, M), jnp....  26.8 us
    unnamed x2, local copies, waits for them, and re-layouts  3.54 us

profile of v1, /device:TPU:1, one launch (start us, length us, event | category | flops | bytes accessed | tf_op | source)
XLA Modules:
  0.0 31.0 jit_solution(18221720341077907521)
XLA Ops:
  0.6 26.8 %shard_map.50 = (f32[4,2,64,64]{3,2,1,0:T(8,128)}, bf16[4,16,4096]{2,1,0:T(8,128)(2,1)}) custom-call(bf16[4,2,32,8192]{3,2,1,0:T(8,128)(2,1)} %spec.1, f32[1,8192]{1,0:T(1,128)} %bitcast.4, f32[4,2,8,64]{3,2,1,0:T(8,128)} %bitcast.5), custom_call_target="tpu_custom_call" | custom-call | tf_op jit(solution)/shard_map/pallas_call | solution.py:239
  27.4 1.7 %copy.7 = f32[4,2,64,64]{3,2,1,0:T(8,128)} copy(f32[4,2,64,64]{3,2,1,0:T(8,128)} %get-tuple-element.8) | data formatting | bytes 262144
  29.1 1.9 %copy.8 = bf16[4,2,8,4096]{3,2,1,0:T(8,128)(2,1)} copy(bf16[4,2,8,4096]{3,2,1,0:T(8,128)(2,1)} %bitcast.3) | data formatting | bytes 1048576

commit v2 on v1

v2 whole, which is shorter than its diff:
```python
import jax
import jax.numpy as jnp
from jax import lax
from jax.experimental import pallas as pl
from jax.experimental.pallas import tpu as pltpu
from jax.sharding import PartitionSpec as P

MESH = pl.DeviceIdType.MESH
K, M, N = 4, 64, 8
NX, NY, NZ = 4, 4, 8
PLANE = NX * NY
BINS = K // 2
HALF = M // 2
ROWS = 48
XY, Z = 0, 1


def ring_distance(d, n):
    return min(d, n - d)


STEPS_XY = sorted(
    ((dx, dy) for dx in range(NX) for dy in range(NY) if dx or dy),
    key=lambda d: -ring_distance(d[0], NX) - ring_distance(d[1], NY),
)
STEPS_Z = sorted(range(1, NZ), key=lambda d: -ring_distance(d, NZ))


def positions():
    return [lax.broadcasted_iota(jnp.int32, (M, 128), d) for d in (0, 1)]


def kernel(
    spec, wts, vec, raw, sums,
    s_all, w, v, mix, raw_away, box_xy, box_z,
    pair, all_in, load_sem, small_sem, swap_send, swap_recv, sum_send, sum_recv, out_send, out_recv,
):
    here = lax.axis_index("space")
    core = lax.axis_index("blk")
    x, y, z = here // (NY * NZ), (here // NZ) % NY, here % NZ
    points = s_all.shape[3]
    share = points // 2
    sibling = (here, 1 - core)
    first = core * BINS
    peers = {
        XY: [((((x + dx) % NX) * NY + (y + dy) % NY) * NZ + z, core) for dx, dy in STEPS_XY],
        Z: [((x * NY + y) * NZ + (z + d) % NZ, core) for d in STEPS_Z],
    }
    boxes = {XY: box_xy, Z: box_z}
    slots = {XY: x * NY + y, Z: z}

    w_copy = pltpu.make_async_copy(wts, w, small_sem.at[0])
    v_copy = pltpu.make_async_copy(vec.at[pl.ds(first, BINS)], v, small_sem.at[1])
    v_copy.start()
    w_copy.start()
    rows = pl.ds(pl.multiple_of(core * HALF, HALF), HALF)
    halves = [
        pl.ds(pl.multiple_of((1 - core) * share, share), share),
        pl.ds(pl.multiple_of(core * share, share), share),
    ]
    loads, swaps = {}, {}
    for k in range(BINS):
        for h, theirs in ((0, 1), (1, 0)):
            cols = halves[h]
            loads[k, h] = pltpu.make_async_copy(
                spec.at[first + k, :, :, cols], s_all.at[k, :, rows, cols], load_sem.at[k, h]
            )
            cols = halves[theirs]
            swaps[k, h] = pltpu.make_async_remote_copy(
                src_ref=spec.at[BINS - first + k, :, :, cols],
                dst_ref=s_all.at[k, :, rows, cols],
                send_sem=swap_send.at[k, h],
                recv_sem=swap_recv.at[k, h],
                device_id=sibling,
                device_id_type=MESH,
            )

    barrier = pltpu.get_barrier_semaphore()

    @pl.when(core == 1)
    def _():
        pl.semaphore_signal(barrier, inc=1, device_id=(here, 0), device_id_type=MESH)

    @pl.when(core == 0)
    def _():
        pl.semaphore_wait(barrier, 1)
        pl.semaphore_signal(pair, inc=1, device_id=(here, 1), device_id_type=MESH)

    @pl.when(core == 1)
    def _():
        pl.semaphore_wait(pair, 1)

    for k in range(BINS):
        for h in range(2):
            swaps[k, h].start()
            loads[k, h].start()

    @pl.when(core == 1)
    def _():
        for t, _ in peers[XY] + peers[Z]:
            pl.semaphore_signal(barrier, inc=1, device_id=(t, 1), device_id_type=MESH)

    v_copy.wait()
    for k in range(BINS):
        re, im = v[k, 0], v[k, 1]
        both = jnp.concatenate(
            [jnp.concatenate([re, -im], axis=1), jnp.concatenate([im, re], axis=1)], axis=0
        )
        high = both.astype(jnp.bfloat16).astype(jnp.float32)
        mix[k] = jnp.concatenate([high, both - high], axis=0).astype(jnp.bfloat16)
    w_copy.wait()

    def products(k):
        total = jnp.zeros((2 * M, 2 * M), jnp.float32)
        power = jnp.zeros((N, 128), jnp.float32)
        mixer = mix[k]
        for h in range(2):
            loads[k, h].wait()
            swaps[k, h].wait_recv()

            s = s_all[k, :, :, halves[h]].reshape(2 * M, share)
            wt = w[:, halves[h]]
            weighted = (s.astype(jnp.float32) * wt).astype(jnp.bfloat16)
            total += lax.dot_general(
                weighted, s, (((1,), (1,)), ((), ())), preferred_element_type=jnp.float32
            )
            r = jnp.dot(mixer, s, preferred_element_type=jnp.float32)
            if h == 0:
                raw_away[k] = r[: 2 * N]
            else:
                raw[first + k] = r[: 2 * N]
            full = r[: 2 * N] + r[2 * N :]
            square = full * full
            square = (square[:N] + square[N:]) * wt
            for g in range(share // 128):
                power += square[:, g * 128 : (g + 1) * 128]
        return total, power

    row, lane = positions()

    def message(packed, power):
        high = power.astype(jnp.bfloat16).astype(jnp.float32)
        return jnp.concatenate([packed, high, power - high], axis=0).astype(jnp.bfloat16)

    def pack(total):
        turned = pltpu.roll(total, M, 1)
        real = total[:M] + turned[M:]
        imag = turned[:M] - total[M:]
        held = jnp.where(row >= lane, real, imag)
        return jnp.where(lane[:HALF] < M, held[:HALF], pltpu.roll(held, M, 1)[HALF:])

    def send(k, axis, what):
        box = boxes[axis].at[k, slots[axis]]
        box[...] = what
        for t in peers[axis]:
            pltpu.make_async_remote_copy(
                src_ref=box,
                dst_ref=box,
                send_sem=sum_send.at[k, axis],
                recv_sem=sum_recv.at[k, axis],
                device_id=t,
                device_id_type=MESH,
            ).start()

    def all_others(k, axis):
        return boxes[axis].at[k, pl.ds(0, len(peers[axis]))]

    def gather(k, axis):
        ref = all_others(k, axis)
        pltpu.make_async_copy(ref, ref, sum_recv.at[k, axis]).wait()
        got = boxes[axis][k].astype(jnp.float32)
        got = jnp.sum(got, axis=0)
        return got[:HALF], got[HALF : HALF + N] + got[HALF + N :]

    def to_sibling(i, ours, target):
        return pltpu.make_async_remote_copy(
            src_ref=ours,
            dst_ref=target,
            send_sem=out_send.at[i],
            recv_sem=out_recv.at[i],
            device_id=sibling,
            device_id_type=MESH,
        )

    outs = []

    def finish(k, packed, power):
        sums[first + k] = jnp.concatenate([packed, power], axis=0)
        outs.append(to_sibling(BINS + k, sums.at[first + k], sums.at[first + k]))
        outs[-1].start()

    total, power = products(0)

    @pl.when(core == 1)
    def _():
        pl.semaphore_wait(barrier, len(STEPS_XY) + len(STEPS_Z))
        pl.semaphore_signal(all_in, inc=1, device_id=(here, 0), device_id_type=MESH)

    @pl.when(core == 0)
    def _():
        pl.semaphore_wait(all_in, 1)

    send(0, XY, message(pack(total), power))
    total, power = products(1)
    send(1, Z, message(pack(total), power))
    for k in range(BINS):
        outs.append(to_sibling(k, raw_away.at[k], raw.at[first + k]))
        outs[-1].start()
    send(0, Z, message(*gather(0, XY)))
    send(1, XY, message(*gather(1, Z)))
    finish(0, *gather(0, Z))
    finish(1, *gather(1, XY))

    for k in range(BINS):
        for h in range(2):
            swaps[k, h].wait_send()
        for axis in (XY, Z):
            ref = all_others(k, axis)
            pltpu.make_async_copy(ref, ref, sum_send.at[k, axis]).wait()
    for copy in outs:
        copy.wait()


def finish_kernel(raw, sums, gram, modes, gram_out, modes_out, sem):
    row, lane = positions()
    copies = []

    def write(i, source, target):
        copies.append(pltpu.make_async_copy(source, target, sem.at[i]))
        copies[-1].start()

    for k in range(K):
        lam = jnp.sum(sums[k, HALF:], axis=1, keepdims=True) / M
        factor = lax.rsqrt(lam + 1e-06)
        factor = jnp.concatenate([factor, factor], axis=0)
        modes_out[k] = (raw[k] * factor).astype(jnp.bfloat16)
        write(k, modes_out.at[k], modes.at[k])
    for k in range(K):
        packed = sums[k, :HALF] / M
        held = jnp.concatenate([packed, pltpu.roll(packed, M, 1)], axis=0)
        across = jnp.concatenate([held, held], axis=0).T[:M]
        real = jnp.where(row >= lane, held, across)
        imag = jnp.where(row < lane, held, jnp.where(row > lane, -across, 0.0))
        gram_out[k, 0] = real[:, :M]
        gram_out[k, 1] = imag[:, :M]
        write(K + k, gram_out.at[k], gram.at[k])
    for copy in copies:
        copy.wait()


def on_device(spectra, weights, vectors):
    points = spectra.shape[3]
    share = points // 2
    dma = pltpu.SemaphoreType.DMA
    vmem = pl.BlockSpec(memory_space=pltpu.VMEM)
    anywhere = pl.BlockSpec(memory_space=pl.ANY)
    raw, sums = pl.pallas_call(
        kernel,
        out_shape=(
            pltpu.VMEM((K, 2 * N, share), jnp.float32),
            pltpu.VMEM((K, HALF + N, 128), jnp.float32),
        ),
        in_specs=[anywhere] * 3,
        out_specs=[vmem] * 2,
        scratch_shapes=[
            pltpu.VMEM((BINS, 2, M, points), jnp.bfloat16),
            pltpu.VMEM((1, points), jnp.float32),
            pltpu.VMEM((BINS, 2, N, M), jnp.float32),
            pltpu.VMEM((BINS, 4 * N, 2 * M), jnp.bfloat16),
            pltpu.VMEM((BINS, 2 * N, share), jnp.float32),
            pltpu.VMEM((BINS, PLANE, ROWS, 128), jnp.bfloat16),
            pltpu.VMEM((BINS, NZ, ROWS, 128), jnp.bfloat16),
            pltpu.SemaphoreType.REGULAR,
            pltpu.SemaphoreType.REGULAR,
            dma((BINS, 2)),
            dma((2,)),
            dma((BINS, 2)),
            dma((BINS, 2)),
            dma((BINS, 2)),
            dma((BINS, 2)),
            dma((2 * BINS,)),
            dma((2 * BINS,)),
        ],
        compiler_params=pltpu.CompilerParams(
            collective_id=0, has_side_effects=True, vmem_limit_bytes=32 * 1024 * 1024
        ),
    )(
        pltpu.with_memory_space_constraint(spectra, pltpu.HBM),
        pltpu.with_memory_space_constraint(weights.reshape(1, points), pltpu.HBM),
        pltpu.with_memory_space_constraint(jnp.swapaxes(vectors, 2, 3), pltpu.HBM),
    )
    gram, modes = pl.pallas_call(
        finish_kernel,
        out_shape=(
            jax.ShapeDtypeStruct((K, 2, M, M), jnp.float32),
            jax.ShapeDtypeStruct((K, 2 * N, share), jnp.bfloat16),
        ),
        in_specs=[vmem] * 2,
        out_specs=[anywhere] * 2,
        scratch_shapes=[
            pltpu.VMEM((K, 2, M, M), jnp.float32),
            pltpu.VMEM((K, 2 * N, share), jnp.bfloat16),
            dma((2 * K,)),
        ],
    )(
        pltpu.with_memory_space_constraint(raw, pltpu.VMEM),
        pltpu.with_memory_space_constraint(sums, pltpu.VMEM),
    )
    return gram, modes.reshape(K, 2, N, share)


def solution(mesh):
    return jax.shard_map(
        on_device,
        mesh=mesh,
        in_specs=(P(None, None, "blk", "space"), P("space"), P()),
        out_specs=(P(), P(None, None, None, ("space", "blk"))),
        check_vma=False,
    )
```

time: 31.2 us -> 27.5 us (0.88)
  local copies, waits for them, and re-layouts: 3.54 us -> 0 us
    unnamed x2 -> x0, local copies, waits for them, and re-layouts: 3.54 us -> none
    pallas_call x1 -> x2, Pallas kernels: 26.8 us -> 26.7 us  [the longest x1 25.6 us: on_device(): pl.pallas_call(kernel, out_shape=(pltpu.VMEM((K, 2 * N, share), jnp.float...]
where the time goes in v2:
time: 27.5 us; the launch traced here: 27.4 us
  Pallas kernels  26.7 us (97%)
  between operations  0.64 us (2%)
    pallas_call x1, Pallas kernels, on_device(): pl.pallas_call(kernel, out_shape=(pltpu.VMEM((K, 2 * N, share), jnp.float...  25.6 us
    pallas_call x1, Pallas kernels, on_device(): pl.pallas_call(finish_kernel, out_shape=(jax.ShapeDtypeStruct((K, 2, M, M...  1.16 us

profile of v2, /device:TPU:1, one launch (start us, length us, event | category | flops | bytes accessed | tf_op | source)
XLA Modules:
  0.0 27.4 jit_solution(11652856012192407051)
XLA Ops:
  0.6 25.6 %shard_map.50 = (f32[4,16,4096]{2,1,0:T(8,128)S(1)}, f32[4,40,128]{2,1,0:T(8,128)S(1)}) custom-call(bf16[4,2,32,8192]{3,2,1,0:T(8,128)(2,1)} %spec.1, f32[1,8192]{1,0:T(1,128)} %bitcast.3, f32[4,2,8,64]{3,2,1,0:T(8,128)} %bitcast.4), custom_call_target="tpu_custom_call" | custom-call | tf_op jit(solution)/shard_map/pallas_call | solution.py:257
  26.2 1.2 %shard_map.51 = (f32[4,2,64,64]{3,2,1,0:T(8,128)}, bf16[4,16,4096]{2,1,0:T(8,128)(2,1)}) custom-call(f32[4,16,4096]{2,1,0:T(8,128)S(1)} %get-tuple-element.6.raw, f32[4,40,128]{2,1,0:T(8,128)S(1)} %get-tuple-element.7.sums), custom_call_target="tpu_custom_call" | custom-call | tf_op jit(solution)/shard_map/pallas_call | solution.py:292

commit v3 on v2

--- a/solution.py
+++ b/solution.py
@@ -12,6 +12,8 @@
 BINS = K // 2
 HALF = M // 2
 ROWS = 48
+SPLIT = 1
+PARTS = 2 * SPLIT
 XY, Z = 0, 1
 
 
@@ -32,8 +34,8 @@
 
 def kernel(
     spec, wts, vec, raw, sums,
-    s_all, w, v, mix, raw_away, box_xy, box_z,
-    pair, all_in, load_sem, small_sem, swap_send, swap_recv, sum_send, sum_recv, out_send, out_recv,
+    s_all, w, v, mix, raw_both, total, power, box_xy, box_z, box_other,
+    pair, all_in, load_sem, small_sem, swap_send, swap_recv, sum_send, sum_recv, other_sem, keep_sem, out_send, out_recv,
 ):
     here = lax.axis_index("space")
     core = lax.axis_index("blk")
@@ -42,58 +44,60 @@
     share = points // 2
     sibling = (here, 1 - core)
     first = core * BINS
-    peers = {
-        XY: [((((x + dx) % NX) * NY + (y + dy) % NY) * NZ + z, core) for dx, dy in STEPS_XY],
-        Z: [((x * NY + y) * NZ + (z + d) % NZ, core) for d in STEPS_Z],
-    }
     boxes = {XY: box_xy, Z: box_z}
     slots = {XY: x * NY + y, Z: z}
+
+    barrier = pltpu.get_barrier_semaphore()
+
+    @pl.when(core == 1)
+    def _():
+        pl.semaphore_signal(barrier, inc=1, device_id=(here, 0), device_id_type=MESH)
+
+    @pl.when(core == 0)
+    def _():
+        pl.semaphore_wait(barrier, 1)
+        pl.semaphore_signal(pair, inc=1, device_id=(here, 1), device_id_type=MESH)
+
+    @pl.when(core == 1)
+    def _():
+        pl.semaphore_wait(pair, 1)
 
     w_copy = pltpu.make_async_copy(wts, w, small_sem.at[0])
     v_copy = pltpu.make_async_copy(vec.at[pl.ds(first, BINS)], v, small_sem.at[1])
     v_copy.start()
     w_copy.start()
     rows = pl.ds(pl.multiple_of(core * HALF, HALF), HALF)
-    halves = [
-        pl.ds(pl.multiple_of((1 - core) * share, share), share),
-        pl.ds(pl.multiple_of(core * share, share), share),
-    ]
-    loads, swaps = {}, {}
+    span = share // SPLIT
+
+    def columns(half, part):
+        return pl.ds(pl.multiple_of(half * share + part * span, span), span)
+
+    def load(k, part):
+        cols = columns(lax.rem(1 - core + part // SPLIT, 2), part % SPLIT)
+        return pltpu.make_async_copy(
+            spec.at[first + k, :, :, cols], s_all.at[k, :, rows, cols], load_sem.at[k, part]
+        )
+
+    def swap(k, part):
+        cols = columns(lax.rem(core + part // SPLIT, 2), part % SPLIT)
+        return pltpu.make_async_remote_copy(
+            src_ref=spec.at[BINS - first + k, :, :, cols],
+            dst_ref=s_all.at[k, :, rows, cols],
+            send_sem=swap_send.at[k, part],
+            recv_sem=swap_recv.at[k, part],
+            device_id=sibling,
+            device_id_type=MESH,
+        )
+
     for k in range(BINS):
-        for h, theirs in ((0, 1), (1, 0)):
-            cols = halves[h]
-            loads[k, h] = pltpu.make_async_copy(
-                spec.at[first + k, :, :, cols], s_all.at[k, :, rows, cols], load_sem.at[k, h]
-            )
-            cols = halves[theirs]
-            swaps[k, h] = pltpu.make_async_remote_copy(
-                src_ref=spec.at[BINS - first + k, :, :, cols],
-                dst_ref=s_all.at[k, :, rows, cols],
-                send_sem=swap_send.at[k, h],
-                recv_sem=swap_recv.at[k, h],
-                device_id=sibling,
-                device_id_type=MESH,
-            )
-
-    barrier = pltpu.get_barrier_semaphore()
-
-    @pl.when(core == 1)
-    def _():
-        pl.semaphore_signal(barrier, inc=1, device_id=(here, 0), device_id_type=MESH)
-
-    @pl.when(core == 0)
-    def _():
-        pl.semaphore_wait(barrier, 1)
-        pl.semaphore_signal(pair, inc=1, device_id=(here, 1), device_id_type=MESH)
-
-    @pl.when(core == 1)
-    def _():
-        pl.semaphore_wait(pair, 1)
-
-    for k in range(BINS):
-        for h in range(2):
-            swaps[k, h].start()
-            loads[k, h].start()
+        for part in range(PARTS):
+            swap(k, part).start()
+            load(k, part).start()
+
+    peers = {
+        XY: [((((x + dx) % NX) * NY + (y + dy) % NY) * NZ + z, core) for dx, dy in STEPS_XY],
+        Z: [((x * NY + y) * NZ + (z + d) % NZ, core) for d in STEPS_Z],
+    }
 
     @pl.when(core == 1)
     def _():
@@ -109,32 +113,6 @@
         high = both.astype(jnp.bfloat16).astype(jnp.float32)
         mix[k] = jnp.concatenate([high, both - high], axis=0).astype(jnp.bfloat16)
     w_copy.wait()
-
-    def products(k):
-        total = jnp.zeros((2 * M, 2 * M), jnp.float32)
-        power = jnp.zeros((N, 128), jnp.float32)
-        mixer = mix[k]
-        for h in range(2):
-            loads[k, h].wait()
-            swaps[k, h].wait_recv()
-
-            s = s_all[k, :, :, halves[h]].reshape(2 * M, share)
-            wt = w[:, halves[h]]
-            weighted = (s.astype(jnp.float32) * wt).astype(jnp.bfloat16)
-            total += lax.dot_general(
-                weighted, s, (((1,), (1,)), ((), ())), preferred_element_type=jnp.float32
-            )
-            r = jnp.dot(mixer, s, preferred_element_type=jnp.float32)
-            if h == 0:
-                raw_away[k] = r[: 2 * N]
-            else:
-                raw[first + k] = r[: 2 * N]
-            full = r[: 2 * N] + r[2 * N :]
-            square = full * full
-            square = (square[:N] + square[N:]) * wt
-            for g in range(share // 128):
-                power += square[:, g * 128 : (g + 1) * 128]
-        return total, power
 
     row, lane = positions()
 
@@ -149,9 +127,20 @@
         held = jnp.where(row >= lane, real, imag)
         return jnp.where(lane[:HALF] < M, held[:HALF], pltpu.roll(held, M, 1)[HALF:])
 
-    def send(k, axis, what):
+    def send(k, axis, what, both=False):
         box = boxes[axis].at[k, slots[axis]]
         box[...] = what
+
+        def other(t):
+            pltpu.make_async_remote_copy(
+                src_ref=box,
+                dst_ref=box_other.at[slots[axis]],
+                send_sem=other_sem.at[0],
+                recv_sem=other_sem.at[1],
+                device_id=(t, 1 - core),
+                device_id_type=MESH,
+            ).start()
+
         for t in peers[axis]:
             pltpu.make_async_remote_copy(
                 src_ref=box,
@@ -161,6 +150,10 @@
                 device_id=t,
                 device_id_type=MESH,
             ).start()
+            if both:
+                other(t[0])
+        if both:
+            other(here)
 
     def all_others(k, axis):
         return boxes[axis].at[k, pl.ds(0, len(peers[axis]))]
@@ -168,8 +161,10 @@
     def gather(k, axis):
         ref = all_others(k, axis)
         pltpu.make_async_copy(ref, ref, sum_recv.at[k, axis]).wait()
-        got = boxes[axis][k].astype(jnp.float32)
-        got = jnp.sum(got, axis=0)
+        return add_up(boxes[axis][k])
+
+    def add_up(got):
+        got = jnp.sum(got.astype(jnp.float32), axis=0)
         return got[:HALF], got[HALF : HALF + N] + got[HALF + N :]
 
     def to_sibling(i, ours, target):
@@ -184,39 +179,67 @@
 
     outs = []
 
-    def finish(k, packed, power):
-        sums[first + k] = jnp.concatenate([packed, power], axis=0)
-        outs.append(to_sibling(BINS + k, sums.at[first + k], sums.at[first + k]))
-        outs[-1].start()
-
-    total, power = products(0)
-
-    @pl.when(core == 1)
-    def _():
-        pl.semaphore_wait(barrier, len(STEPS_XY) + len(STEPS_Z))
-        pl.semaphore_signal(all_in, inc=1, device_id=(here, 0), device_id_type=MESH)
-
-    @pl.when(core == 0)
-    def _():
-        pl.semaphore_wait(all_in, 1)
-
-    send(0, XY, message(pack(total), power))
-    total, power = products(1)
-    send(1, Z, message(pack(total), power))
+    def finish(at, packed, power):
+        sums[at] = jnp.concatenate([packed, power], axis=0)
+
+    total[...] = jnp.zeros_like(total)
+    power[...] = jnp.zeros_like(power)
+
+    @pl.loop(0, BINS * PARTS)
+    def _(i):
+        k, part = i // PARTS, i % PARTS
+        cols = columns(lax.rem(1 - core + part // SPLIT, 2), part % SPLIT)
+        load(k, part).wait()
+        swap(k, part).wait_recv()
+        s = s_all[k, :, :, cols].reshape(2 * M, span)
+        wt = w[:, cols]
+        weighted = (s.astype(jnp.float32) * wt).astype(jnp.bfloat16)
+        total[k] += lax.dot_general(
+            weighted, s, (((1,), (1,)), ((), ())), preferred_element_type=jnp.float32
+        )
+        r = jnp.dot(mix[k], s, preferred_element_type=jnp.float32)
+        raw_both[k, part // SPLIT, :, pl.ds(pl.multiple_of(part % SPLIT * span, span), span)] = r[: 2 * N]
+        full = r[: 2 * N] + r[2 * N :]
+        square = full * full
+        square = (square[:N] + square[N:]) * wt
+        power[k] += sum(square[:, g : g + 128] for g in range(0, span, 128))
+
+        @pl.when(i == PARTS - 1)
+        def _():
+            @pl.when(core == 1)
+            def _():
+                pl.semaphore_wait(barrier, len(STEPS_XY) + len(STEPS_Z))
+                pl.semaphore_signal(all_in, inc=1, device_id=(here, 0), device_id_type=MESH)
+
+            @pl.when(core == 0)
+            def _():
+                pl.semaphore_wait(all_in, 1)
+
+            send(0, XY, message(pack(total[0]), power[0]))
+
+    send(1, Z, message(pack(total[1]), power[1]))
     for k in range(BINS):
-        outs.append(to_sibling(k, raw_away.at[k], raw.at[first + k]))
+        keep = pltpu.make_async_copy(raw_both.at[k, 1], raw.at[first + k], keep_sem.at[k])
+        keep.start()
+        outs.append(keep)
+        outs.append(to_sibling(k, raw_both.at[k, 0], raw.at[first + k]))
         outs[-1].start()
     send(0, Z, message(*gather(0, XY)))
-    send(1, XY, message(*gather(1, Z)))
-    finish(0, *gather(0, Z))
-    finish(1, *gather(1, XY))
+    send(1, XY, message(*gather(1, Z)), both=True)
+    finish(first, *gather(0, Z))
+    outs.append(to_sibling(BINS, sums.at[first], sums.at[first]))
+    outs[-1].start()
+    finish(first + 1, *gather(1, XY))
+    pltpu.make_async_copy(box_other, box_other, other_sem.at[1]).wait()
+    finish(BINS - first + 1, *add_up(box_other[...]))
 
     for k in range(BINS):
-        for h in range(2):
-            swaps[k, h].wait_send()
+        for part in range(PARTS):
+            swap(k, part).wait_send()
         for axis in (XY, Z):
             ref = all_others(k, axis)
             pltpu.make_async_copy(ref, ref, sum_send.at[k, axis]).wait()
+    pltpu.make_async_copy(box_other, box_other, other_sem.at[0]).wait()
     for copy in outs:
         copy.wait()
 
@@ -267,19 +290,24 @@
             pltpu.VMEM((1, points), jnp.float32),
             pltpu.VMEM((BINS, 2, N, M), jnp.float32),
             pltpu.VMEM((BINS, 4 * N, 2 * M), jnp.bfloat16),
-            pltpu.VMEM((BINS, 2 * N, share), jnp.float32),
+            pltpu.VMEM((BINS, 2, 2 * N, share), jnp.float32),
+            pltpu.VMEM((BINS, 2 * M, 2 * M), jnp.float32),
+            pltpu.VMEM((BINS, N, 128), jnp.float32),
             pltpu.VMEM((BINS, PLANE, ROWS, 128), jnp.bfloat16),
             pltpu.VMEM((BINS, NZ, ROWS, 128), jnp.bfloat16),
+            pltpu.VMEM((PLANE, ROWS, 128), jnp.bfloat16),
             pltpu.SemaphoreType.REGULAR,
             pltpu.SemaphoreType.REGULAR,
+            dma((BINS, PARTS)),
+            dma((2,)),
+            dma((BINS, PARTS)),
+            dma((BINS, PARTS)),
+            dma((BINS, 2)),
             dma((BINS, 2)),
             dma((2,)),
-            dma((BINS, 2)),
-            dma((BINS, 2)),
-            dma((BINS, 2)),
-            dma((BINS, 2)),
-            dma((2 * BINS,)),
-            dma((2 * BINS,)),
+            dma((BINS,)),
+            dma((BINS + 1,)),
+            dma((BINS + 1,)),
         ],
         compiler_params=pltpu.CompilerParams(
             collective_id=0, has_side_effects=True, vmem_limit_bytes=32 * 1024 * 1024

time: 27.5 us -> 26 us (0.945)
  Pallas kernels: 26.7 us -> 25.2 us
    pallas_call x1, Pallas kernels: 25.6 us -> 24 us  [on_device(): pl.pallas_call(kernel, out_shape=(pltpu.VMEM((K, 2 * N, share), jnp.float...]
where the time goes in v3:
time: 26 us; the launch traced here: 25.8 us
  Pallas kernels  25.2 us (97%)
  between operations  0.64 us (2%)
    pallas_call x1, Pallas kernels, on_device(): pl.pallas_call(kernel, out_shape=(pltpu.VMEM((K, 2 * N, share), jnp.float...  24 us
    pallas_call x1, Pallas kernels, on_device(): pl.pallas_call(finish_kernel, out_shape=(jax.ShapeDtypeStruct((K, 2, M, M...  1.16 us

profile of v3, /device:TPU:1, one launch (start us, length us, event | category | flops | bytes accessed | tf_op | source)
XLA Modules:
  0.0 25.8 jit_solution(17714957856383092304)
XLA Ops:
  0.6 24.0 %shard_map.50 = (f32[4,16,4096]{2,1,0:T(8,128)S(1)}, f32[4,40,128]{2,1,0:T(8,128)S(1)}) custom-call(bf16[4,2,32,8192]{3,2,1,0:T(8,128)(2,1)} %spec.1, f32[1,8192]{1,0:T(1,128)} %bitcast.3, f32[4,2,8,64]{3,2,1,0:T(8,128)} %bitcast.4), custom_call_target="tpu_custom_call" | custom-call | tf_op jit(solution)/shard_map/pallas_call | solution.py:280
  24.7 1.2 %shard_map.51 = (f32[4,2,64,64]{3,2,1,0:T(8,128)}, bf16[4,16,4096]{2,1,0:T(8,128)(2,1)}) custom-call(f32[4,16,4096]{2,1,0:T(8,128)S(1)} %get-tuple-element.6.raw, f32[4,40,128]{2,1,0:T(8,128)S(1)} %get-tuple-element.7.sums), custom_call_target="tpu_custom_call" | custom-call | tf_op jit(solution)/shard_map/pallas_call | solution.py:320

commit v4 on v3

--- a/solution.py
+++ b/solution.py
@@ -32,9 +32,25 @@
     return [lax.broadcasted_iota(jnp.int32, (M, 128), d) for d in (0, 1)]
 
 
+def unpack(packed):
+    row, lane = positions()
+    packed = packed / M
+    held = jnp.concatenate([packed, pltpu.roll(packed, M, 1)], axis=0)
+    across = jnp.concatenate([held, held], axis=0).T[:M]
+    real = jnp.where(row >= lane, held, across)
+    imag = jnp.where(row < lane, held, jnp.where(row > lane, -across, 0.0))
+    return real[:, :M], imag[:, :M]
+
+
+def scale(power):
+    lam = jnp.sum(power, axis=1, keepdims=True) / M
+    factor = lax.rsqrt(lam + 1e-06)
+    return jnp.concatenate([factor, factor], axis=0)
+
+
 def kernel(
-    spec, wts, vec, raw, sums,
-    s_all, w, v, mix, raw_both, total, power, box_xy, box_z, box_other,
+    spec, wts, vec, raw, sums, modes_early, gram_early,
+    s_all, w, v, mix, raw_both, raw_early, sums_early, total, power, box_xy, box_z, box_other,
     pair, all_in, load_sem, small_sem, swap_send, swap_recv, sum_send, sum_recv, other_sem, keep_sem, out_send, out_recv,
 ):
     here = lax.axis_index("space")
@@ -177,10 +193,12 @@
             device_id_type=MESH,
         )
 
-    outs = []
-
-    def finish(at, packed, power):
-        sums[at] = jnp.concatenate([packed, power], axis=0)
+    def keep(where, packed, power):
+        where[...] = jnp.concatenate([packed, power], axis=0)
+
+    def finish_early(at, unscaled):
+        modes_early[at] = (unscaled * scale(sums_early[at, HALF:])).astype(jnp.bfloat16)
+        gram_early[at, 0], gram_early[at, 1] = unpack(sums_early[at, :HALF])
 
     total[...] = jnp.zeros_like(total)
     power[...] = jnp.zeros_like(power)
@@ -218,20 +236,23 @@
             send(0, XY, message(pack(total[0]), power[0]))
 
     send(1, Z, message(pack(total[1]), power[1]))
-    for k in range(BINS):
-        keep = pltpu.make_async_copy(raw_both.at[k, 1], raw.at[first + k], keep_sem.at[k])
-        keep.start()
-        outs.append(keep)
-        outs.append(to_sibling(k, raw_both.at[k, 0], raw.at[first + k]))
-        outs[-1].start()
+    own_raw = pltpu.make_async_copy(raw_both.at[1, 1], raw.at[core], keep_sem)
+    early_raw = to_sibling(0, raw_both.at[0, 0], raw_early)
+    late_raw = to_sibling(1, raw_both.at[1, 0], raw.at[core])
+    for copy in (early_raw, late_raw, own_raw):
+        copy.start()
     send(0, Z, message(*gather(0, XY)))
     send(1, XY, message(*gather(1, Z)), both=True)
-    finish(first, *gather(0, Z))
-    outs.append(to_sibling(BINS, sums.at[first], sums.at[first]))
-    outs[-1].start()
-    finish(first + 1, *gather(1, XY))
+    keep(sums_early.at[core], *gather(0, Z))
+    early_sums = to_sibling(2, sums_early.at[core], sums_early.at[core])
+    early_sums.start()
+    finish_early(core, raw_both[0, 1])
+    early_sums.wait()
+    early_raw.wait()
+    finish_early(1 - core, raw_early[...])
+    keep(sums.at[core], *gather(1, XY))
     pltpu.make_async_copy(box_other, box_other, other_sem.at[1]).wait()
-    finish(BINS - first + 1, *add_up(box_other[...]))
+    keep(sums.at[1 - core], *add_up(box_other[...]))
 
     for k in range(BINS):
         for part in range(PARTS):
@@ -240,33 +261,26 @@
             ref = all_others(k, axis)
             pltpu.make_async_copy(ref, ref, sum_send.at[k, axis]).wait()
     pltpu.make_async_copy(box_other, box_other, other_sem.at[0]).wait()
-    for copy in outs:
-        copy.wait()
-
-
-def finish_kernel(raw, sums, gram, modes, gram_out, modes_out, sem):
-    row, lane = positions()
+    late_raw.wait()
+    own_raw.wait()
+
+
+def finish_kernel(raw, sums, modes_early, gram_early, gram, modes, gram_out, modes_out, sem):
     copies = []
 
-    def write(i, source, target):
-        copies.append(pltpu.make_async_copy(source, target, sem.at[i]))
+    def write(source, target):
+        copies.append(pltpu.make_async_copy(source, target, sem.at[len(copies)]))
         copies[-1].start()
 
-    for k in range(K):
-        lam = jnp.sum(sums[k, HALF:], axis=1, keepdims=True) / M
-        factor = lax.rsqrt(lam + 1e-06)
-        factor = jnp.concatenate([factor, factor], axis=0)
-        modes_out[k] = (raw[k] * factor).astype(jnp.bfloat16)
-        write(k, modes_out.at[k], modes.at[k])
-    for k in range(K):
-        packed = sums[k, :HALF] / M
-        held = jnp.concatenate([packed, pltpu.roll(packed, M, 1)], axis=0)
-        across = jnp.concatenate([held, held], axis=0).T[:M]
-        real = jnp.where(row >= lane, held, across)
-        imag = jnp.where(row < lane, held, jnp.where(row > lane, -across, 0.0))
-        gram_out[k, 0] = real[:, :M]
-        gram_out[k, 1] = imag[:, :M]
-        write(K + k, gram_out.at[k], gram.at[k])
+    for c in range(2):
+        write(modes_early.at[c], modes.at[BINS * c])
+        write(gram_early.at[c], gram.at[BINS * c])
+    for c in range(2):
+        modes_out[c] = (raw[c] * scale(sums[c, HALF:])).astype(jnp.bfloat16)
+        write(modes_out.at[c], modes.at[BINS * c + 1])
+    for c in range(2):
+        gram_out[c, 0], gram_out[c, 1] = unpack(sums[c, :HALF])
+        write(gram_out.at[c], gram.at[BINS * c + 1])
     for copy in copies:
         copy.wait()
 
@@ -277,20 +291,24 @@
     dma = pltpu.SemaphoreType.DMA
     vmem = pl.BlockSpec(memory_space=pltpu.VMEM)
     anywhere = pl.BlockSpec(memory_space=pl.ANY)
-    raw, sums = pl.pallas_call(
+    early = pl.pallas_call(
         kernel,
         out_shape=(
-            pltpu.VMEM((K, 2 * N, share), jnp.float32),
-            pltpu.VMEM((K, HALF + N, 128), jnp.float32),
+            pltpu.VMEM((2, 2 * N, share), jnp.float32),
+            pltpu.VMEM((2, HALF + N, 128), jnp.float32),
+            pltpu.VMEM((2, 2 * N, share), jnp.bfloat16),
+            pltpu.VMEM((2, 2, M, M), jnp.float32),
         ),
         in_specs=[anywhere] * 3,
-        out_specs=[vmem] * 2,
+        out_specs=[vmem] * 4,
         scratch_shapes=[
             pltpu.VMEM((BINS, 2, M, points), jnp.bfloat16),
             pltpu.VMEM((1, points), jnp.float32),
             pltpu.VMEM((BINS, 2, N, M), jnp.float32),
             pltpu.VMEM((BINS, 4 * N, 2 * M), jnp.bfloat16),
             pltpu.VMEM((BINS, 2, 2 * N, share), jnp.float32),
+            pltpu.VMEM((2 * N, share), jnp.float32),
+            pltpu.VMEM((2, HALF + N, 128), jnp.float32),
             pltpu.VMEM((BINS, 2 * M, 2 * M), jnp.float32),
             pltpu.VMEM((BINS, N, 128), jnp.float32),
             pltpu.VMEM((BINS, PLANE, ROWS, 128), jnp.bfloat16),
@@ -305,9 +323,9 @@
             dma((BINS, 2)),
             dma((BINS, 2)),
             dma((2,)),
-            dma((BINS,)),
-            dma((BINS + 1,)),
-            dma((BINS + 1,)),
+            dma,
+            dma((3,)),
+            dma((3,)),
         ],
         compiler_params=pltpu.CompilerParams(
             collective_id=0, has_side_effects=True, vmem_limit_bytes=32 * 1024 * 1024
@@ -323,17 +341,14 @@
             jax.ShapeDtypeStruct((K, 2, M, M), jnp.float32),
             jax.ShapeDtypeStruct((K, 2 * N, share), jnp.bfloat16),
         ),
-        in_specs=[vmem] * 2,
+        in_specs=[vmem] * 4,
         out_specs=[anywhere] * 2,
         scratch_shapes=[
-            pltpu.VMEM((K, 2, M, M), jnp.float32),
-            pltpu.VMEM((K, 2 * N, share), jnp.bfloat16),
+            pltpu.VMEM((2, 2, M, M), jnp.float32),
+            pltpu.VMEM((2, 2 * N, share), jnp.bfloat16),
             dma((2 * K,)),
         ],
-    )(
-        pltpu.with_memory_space_constraint(raw, pltpu.VMEM),
-        pltpu.with_memory_space_constraint(sums, pltpu.VMEM),
-    )
+    )(*(pltpu.with_memory_space_constraint(a, pltpu.VMEM) for a in early))
     return gram, modes.reshape(K, 2, N, share)
 
 

time: 26 us -> 25.8 us (level)
  no operation moved by 1% of the time
where the time goes in v4:
time: 25.8 us; the launch traced here: 25.7 us
  Pallas kernels  25 us (97%)
  between operations  0.64 us (2%)
    pallas_call x1, Pallas kernels, on_device(): pl.pallas_call(kernel, out_shape=(pltpu.VMEM((2, 2 * N, share), jnp.float...  24 us
    pallas_call x1, Pallas kernels, on_device(): pl.pallas_call(finish_kernel, out_shape=(jax.ShapeDtypeStruct((K, 2, M, M...  1 us

profile of v4, /device:TPU:1, one launch (start us, length us, event | category | flops | bytes accessed | tf_op | source)
XLA Modules:
  0.0 25.7 jit_solution(13769338573241300915)
XLA Ops:
  0.6 24.0 %shard_map.50 = (f32[2,16,4096]{2,1,0:T(8,128)S(1)}, f32[2,40,128]{2,1,0:T(8,128)S(1)}, bf16[2,16,4096]{2,1,0:T(8,128)(2,1)S(1)}, f32[2,2,64,64]{3,2,1,0:T(8,128)S(1)}) custom-call(bf16[4,2,32,8192]{3,2,1,0:T(8,128)(2,1)} %spec.1, f32[1,8192]{1,0:T(1,128)} %bitcast.3, f32[4,2,8,64]{3,2,1,0:T(8,128)} %bitcast.4), custom_call_target="tpu_custom_call" | custom-call | tf_op jit(solution)/shard_map/pallas_call | solution.py:294
  24.7 1.0 %shard_map.51 = (f32[4,2,64,64]{3,2,1,0:T(8,128)}, bf16[4,16,4096]{2,1,0:T(8,128)(2,1)}) custom-call(f32[2,16,4096]{2,1,0:T(8,128)S(1)} %get-tuple-element.8.raw, f32[2,40,128]{2,1,0:T(8,128)S(1)} %get-tuple-element.9.sums, bf16[2,16,4096]{2,1,0:T(8,128)(2,1)S(1)} %get-tuple-element.10.modes_early, f32[2,2,64,64]{3,2,1,0:T(8,128)S(1)} %get-tuple-element.11.gram_early), custom_call_target="tpu_custom_call" | custom-call | tf_op jit(solution)/shard_map/pallas_call | solution.py:338

commit v5 on v4

--- a/solution.py
+++ b/solution.py
@@ -157,6 +157,9 @@
                 device_id_type=MESH,
             ).start()
 
+        if both:
+            for t, _ in peers[axis]:
+                other(t)
         for t in peers[axis]:
             pltpu.make_async_remote_copy(
                 src_ref=box,
@@ -166,8 +169,6 @@
                 device_id=t,
                 device_id_type=MESH,
             ).start()
-            if both:
-                other(t[0])
         if both:
             other(here)
 

time: 25.8 us -> 25.3 us (0.981)
  Pallas kernels: 25 us -> 24.5 us
    pallas_call x1, Pallas kernels: 24 us -> 23.5 us  [on_device(): pl.pallas_call(kernel, out_shape=(pltpu.VMEM((2, 2 * N, share), jnp.float...]
where the time goes in v5:
time: 25.3 us; the launch traced here: 25.2 us
  Pallas kernels  24.5 us (97%)
  between operations  0.64 us (3%)
    pallas_call x1, Pallas kernels, on_device(): pl.pallas_call(kernel, out_shape=(pltpu.VMEM((2, 2 * N, share), jnp.float...  23.5 us
    pallas_call x1, Pallas kernels, on_device(): pl.pallas_call(finish_kernel, out_shape=(jax.ShapeDtypeStruct((K, 2, M, M...  1 us

profile of v5, /device:TPU:1, one launch (start us, length us, event | category | flops | bytes accessed | tf_op | source)
XLA Modules:
  0.0 25.2 jit_solution(6321419827136772354)
XLA Ops:
  0.6 23.5 %shard_map.50 = (f32[2,16,4096]{2,1,0:T(8,128)S(1)}, f32[2,40,128]{2,1,0:T(8,128)S(1)}, bf16[2,16,4096]{2,1,0:T(8,128)(2,1)S(1)}, f32[2,2,64,64]{3,2,1,0:T(8,128)S(1)}) custom-call(bf16[4,2,32,8192]{3,2,1,0:T(8,128)(2,1)} %spec.1, f32[1,8192]{1,0:T(1,128)} %bitcast.3, f32[4,2,8,64]{3,2,1,0:T(8,128)} %bitcast.4), custom_call_target="tpu_custom_call" | custom-call | tf_op jit(solution)/shard_map/pallas_call | solution.py:295
  24.2 1.0 %shard_map.51 = (f32[4,2,64,64]{3,2,1,0:T(8,128)}, bf16[4,16,4096]{2,1,0:T(8,128)(2,1)}) custom-call(f32[2,16,4096]{2,1,0:T(8,128)S(1)} %get-tuple-element.8.raw, f32[2,40,128]{2,1,0:T(8,128)S(1)} %get-tuple-element.9.sums, bf16[2,16,4096]{2,1,0:T(8,128)(2,1)S(1)} %get-tuple-element.10.modes_early, f32[2,2,64,64]{3,2,1,0:T(8,128)S(1)} %get-tuple-element.11.gram_early), custom_call_target="tpu_custom_call" | custom-call | tf_op jit(solution)/shard_map/pallas_call | solution.py:339

commit v6 on v5

--- a/solution.py
+++ b/solution.py
@@ -240,10 +240,10 @@
     own_raw = pltpu.make_async_copy(raw_both.at[1, 1], raw.at[core], keep_sem)
     early_raw = to_sibling(0, raw_both.at[0, 0], raw_early)
     late_raw = to_sibling(1, raw_both.at[1, 0], raw.at[core])
+    send(0, Z, message(*gather(0, XY)))
+    send(1, XY, message(*gather(1, Z)), both=True)
     for copy in (early_raw, late_raw, own_raw):
         copy.start()
-    send(0, Z, message(*gather(0, XY)))
-    send(1, XY, message(*gather(1, Z)), both=True)
     keep(sums_early.at[core], *gather(0, Z))
     early_sums = to_sibling(2, sums_early.at[core], sums_early.at[core])
     early_sums.start()
@@ -251,9 +251,9 @@
     early_sums.wait()
     early_raw.wait()
     finish_early(1 - core, raw_early[...])
-    keep(sums.at[core], *gather(1, XY))
     pltpu.make_async_copy(box_other, box_other, other_sem.at[1]).wait()
     keep(sums.at[1 - core], *add_up(box_other[...]))
+    keep(sums.at[core], *gather(1, XY))
 
     for k in range(BINS):
         for part in range(PARTS):

time: 25.3 us -> 25.4 us (level)
  no operation moved by 1% of the time
where the time goes in v6:
time: 25.4 us; the launch traced here: 25.2 us
  Pallas kernels  24.6 us (97%)
  between operations  0.64 us (3%)
    pallas_call x1, Pallas kernels, on_device(): pl.pallas_call(kernel, out_shape=(pltpu.VMEM((2, 2 * N, share), jnp.float...  23.6 us
    pallas_call x1, Pallas kernels, on_device(): pl.pallas_call(finish_kernel, out_shape=(jax.ShapeDtypeStruct((K, 2, M, M...  1 us

profile of v6, /device:TPU:1, one launch (start us, length us, event | category | flops | bytes accessed | tf_op | source)
XLA Modules:
  0.0 25.2 jit_solution(6387673555911573296)
XLA Ops:
  0.6 23.6 %shard_map.50 = (f32[2,16,4096]{2,1,0:T(8,128)S(1)}, f32[2,40,128]{2,1,0:T(8,128)S(1)}, bf16[2,16,4096]{2,1,0:T(8,128)(2,1)S(1)}, f32[2,2,64,64]{3,2,1,0:T(8,128)S(1)}) custom-call(bf16[4,2,32,8192]{3,2,1,0:T(8,128)(2,1)} %spec.1, f32[1,8192]{1,0:T(1,128)} %bitcast.3, f32[4,2,8,64]{3,2,1,0:T(8,128)} %bitcast.4), custom_call_target="tpu_custom_call" | custom-call | tf_op jit(solution)/shard_map/pallas_call | solution.py:295
  24.2 1.0 %shard_map.51 = (f32[4,2,64,64]{3,2,1,0:T(8,128)}, bf16[4,16,4096]{2,1,0:T(8,128)(2,1)}) custom-call(f32[2,16,4096]{2,1,0:T(8,128)S(1)} %get-tuple-element.8.raw, f32[2,40,128]{2,1,0:T(8,128)S(1)} %get-tuple-element.9.sums, bf16[2,16,4096]{2,1,0:T(8,128)(2,1)S(1)} %get-tuple-element.10.modes_early, f32[2,2,64,64]{3,2,1,0:T(8,128)S(1)} %get-tuple-element.11.gram_early), custom_call_target="tpu_custom_call" | custom-call | tf_op jit(solution)/shard_map/pallas_call | solution.py:339
